TPU v7x, 32 devices: a whole 2x2x4 slice. The times are simulated.
32 devices in a mesh: groups: 2 (over y), segment: 8 (over z, x), space: 2 (over core).
Axes of the slice: x: 2, y: 2, z: 4, core: 2. Of those that a mesh axis runs over, the one named last changes fastest.
Arguments:
- patches: bfloat16 [16, 256, 1536], P(('groups', 'segment'), 'space'), parts along dimension 0, may hold values from -120 to 120
- positions: int32 [16], P(('groups', 'segment')), parts along dimension 0, may hold values from 0 to 1
- timesteps: int32 [16], P(('groups', 'segment')), parts along dimension 0, may hold values from 0 to 1
- section_bounds: int32 [9], replicated, may hold values from 0 to 12, as said below
- tile_neighbours: int32 [4, 2], replicated, may hold values from 0 to 3, as said below
- modulation: bfloat16 [6, 12, 3, 1536], P('groups'), parts along dimension 0, may hold values from -9 to 9
- query_gain: float32 [12, 128], replicated, may hold values from 0.5 to 2
- stale_kv: bfloat16 [16, 2, 2, 512, 1536], P(('groups', 'segment'), None, None, 'space'), parts along dimension 0, may hold values from -70 to 70
Outputs:
- advanced: bfloat16 [16, 256, 1536], P(('groups', 'segment'), 'space'), parts along dimension 0
There are 2 independent parts, one for each index of `groups`. A program takes and returns all parts, laid end to end along the dimension named above; an argument that names none is the same for every part. Nothing has to cross between parts.
Inputs may be any that keep to these rules, and one draw needn't show every extreme that they name: section_bounds[0] is 0 and section_bounds[8] is 12; section j holds layers section_bounds[j] to section_bounds[j+1] - 1, one or 2 of them, and some sections hold 2. `tile_neighbours`: tile g lies in time layer g // 2; row g names first a tile of its own time layer, then a tile of the other time layer.
All inputs are finite; a program needn't handle non-finite values.
Results may differ from a plain program's by a relative error of at most 0.0051.
Values may be sent and summed in bfloat16 or wider, within the bound.
A program may use at most 64 MiB of HBM per device.

v0:
```python
import jax
import jax.numpy as jnp
from jax import lax
from jax.sharding import PartitionSpec as P

HEADS = 12
HDIM = 128
D = 1536
TILE = 128
SLAB_DEV = 2
NB = 2
PIPE = 8
LMAX = 2
LAYERS = 12
STEPS = 3
TICKS = 2


epsilon = 1e-06


def extended_2(x, sides, width):
    for axis, dim in sides:
        devices, length = (lax.axis_size(axis), x.shape[dim])
        up = [(i, (i + 1) % devices) for i in range(devices - 1)]
        down = [(j, i) for i, j in up]
        last = lax.slice_in_dim(x, length - width, length, axis=dim)
        initial = lax.slice_in_dim(x, 0, width, axis=dim)
        before = lax.ppermute(last, axis, up)
        after = lax.ppermute(initial, axis, down)
        x = jnp.concatenate([before, x, after], axis=dim)
    return x


def from_behind(x, axis, by):
    devices = lax.axis_size(axis)
    return lax.ppermute(x, axis, [(i, (i + by) % devices) for i in range(devices)])


def attend(stream, key_tiles, value_tiles, tile_choice, mod_rows, gain_row):
    batch_size = stream.shape[0]
    middle = jnp.mean(stream, axis=-1, keepdims=True)
    centred = stream - middle
    spread = jnp.mean(centred * centred, axis=-1, keepdims=True)
    normed = centred * lax.rsqrt(spread + epsilon)
    shifted = normed * (1.0 + mod_rows[:, 1:2, :]) + mod_rows[:, 0:1, :]
    heads_in = shifted.reshape(batch_size, TILE, HEADS, HDIM)
    head_rms = jnp.mean(heads_in * heads_in, axis=-1, keepdims=True)
    queries = (heads_in * lax.rsqrt(head_rms + epsilon) * gain_row).astype(jnp.bfloat16)
    key_rows = key_tiles[tile_choice].reshape(batch_size, NB * TILE, HEADS, HDIM)
    value_rows = value_tiles[tile_choice].reshape(batch_size, NB * TILE, HEADS, HDIM)
    scores = jnp.einsum(
        "bqhd,bkhd->bhqk", queries, key_rows, preferred_element_type=jnp.float32
    ) * HDIM ** (-0.5)
    row_max = jnp.max(scores, axis=-1, keepdims=True)
    powers = jnp.exp(scores - row_max)
    totals = jnp.sum(powers, axis=-1)
    weights = powers.astype(jnp.bfloat16)
    blended = jnp.einsum("bhqk,bkhd->bqhd", weights, value_rows, preferred_element_type=jnp.float32)
    blended = blended / jnp.transpose(totals, (0, 2, 1))[..., None]
    return stream + mod_rows[:, 2:3, :] * blended.reshape(batch_size, TILE, D)


def run_slots(holding, ext_index, step_onehot, extended, slot_mods, slot_gains, layer_count):
    stream = holding.astype(jnp.float32)
    for slot_index in range(LMAX):
        mod_rows = jnp.einsum("bs,sjd->bjd", step_onehot, slot_mods[slot_index].astype(jnp.float32))
        updated = attend(
            stream,
            extended[slot_index, 0],
            extended[slot_index, 1],
            ext_index,
            mod_rows,
            slot_gains[slot_index],
        )
        stream = jnp.where(slot_index < layer_count, updated, stream)
    return stream.astype(jnp.bfloat16)


def per_device(
    patches, positions, timesteps, section_bounds, tile_neighbours, modulation, query_gain, stale_kv
):
    tile_len = patches.shape[1]
    feature_width = patches.shape[2]
    local_kv = stale_kv[0]
    framed = extended_2(local_kv[:, :, None], (("space", 2),), 1)
    extended = framed.reshape(LMAX, 2, 3 * SLAB_DEV, tile_len, feature_width)
    device = lax.axis_index("segment")
    space_index = lax.axis_index("space")
    cycle_size = lax.axis_size("segment")
    section = device % PIPE
    first_layer = section_bounds[section]
    layer_count = section_bounds[section + 1] - first_layer
    slot_mods = []
    slot_gains = []
    for slot_index in range(LMAX):
        layer_now = jnp.minimum(first_layer + slot_index, LAYERS - 1)
        slot_mods.append(lax.dynamic_index_in_dim(modulation, layer_now, 1, False))
        slot_gains.append(lax.dynamic_index_in_dim(query_gain, layer_now, 0, False))
    step_range = jnp.arange(STEPS, dtype=jnp.int32)
    holding = patches
    held_pos = positions
    held_steps = timesteps
    for tick_index in range(TICKS):
        if tick_index > 0:
            held_pos, held_steps = from_behind((held_pos, held_steps), "segment", 1)
        root = (device - tick_index) % cycle_size
        step_rows = held_steps + (root % PIPE + tick_index >= PIPE).astype(jnp.int32)
        listed_tiles = tile_neighbours[space_index * SLAB_DEV + held_pos]
        ext_index = (
            listed_tiles // SLAB_DEV - space_index + 1
        ) * SLAB_DEV + listed_tiles % SLAB_DEV
        step_onehot = (step_rows[:, None] == step_range[None, :]).astype(jnp.float32)
        finished = run_slots(
            holding, ext_index, step_onehot, extended, slot_mods, slot_gains, layer_count
        )
        holding = from_behind(finished, "segment", 1)
    return holding


def solution(mesh):
    placed = (
        P(("groups", "segment"), "space", None),
        P(("groups", "segment")),
        P(("groups", "segment")),
        P(),
        P(),
        P("groups", None, None, None),
        P(),
        P(("groups", "segment"), None, None, "space", None),
    )
    return jax.shard_map(
        per_device,
        mesh=mesh,
        in_specs=placed,
        out_specs=P(("groups", "segment"), "space", None),
        check_vma=False,
    )
```

profile of v0, /device:TPU:0, one launch (start us, length us, event | category | flops | bytes accessed | tf_op | source)
XLA Modules:
  0.0 122.3 jit_solution(10010308473332576144)
XLA Ops:
  0.0 1.3 %collective-permute-start.1 = (bf16[2,2,1,256,1536]{4,3,2,1,0:T(8,128)(2,1)}, bf16[2,2,1,256,1536]{4,3,2,1,0:T(8,128)(2,1)}, u32[]{:S(2)}, u32[]{:S(2)}) collective-permute-start(bf16[2,2,1,256,1536]{4,3,2,1,0:T(8,128)(2,1)} %bitcast.236), channel_id=1, source_target_pairs={{1,0},{3,2},{5,4},{7,6},{9,8},{11,10},{13,12},{15,14},{17,16},{19,... | collective-permute-start | bytes 9437192 | tf_op jit(solution)/shard_map/ppermute | solution.py:30
  1.3 6.3 %collective-permute-start = (bf16[2,2,1,256,1536]{4,3,2,1,0:T(8,128)(2,1)}, bf16[2,2,1,256,1536]{4,3,2,1,0:T(8,128)(2,1)}, u32[]{:S(2)}, u32[]{:S(2)}) collective-permute-start(bf16[2,2,1,256,1536]{4,3,2,1,0:T(8,128)(2,1)} %bitcast.237), channel_id=1, source_target_pairs={{0,1},{2,3},{4,5},{6,7},{8,9},{10,11},{12,13},{14,15},{16,17},{18,... | collective-permute-start | bytes 9437192 | tf_op jit(solution)/shard_map/ppermute | solution.py:29
  7.6 2.9 %collective-permute-start.4 = (s32[1]{0:T(128)}, s32[1]{0:T(128)}, u32[]{:S(2)}, u32[]{:S(2)}) collective-permute-start(s32[1]{0:T(128)} %param.9), channel_id=1, source_target_pairs={{0,2},{2,4},{4,6},{6,8},{8,10},{10,12},{12,14},{14,0},{1,3},{3,5},... | collective-permute-start | bytes 20 | tf_op jit(solution)/shard_map/ppermute | solution.py:37
  10.6 1.5 %collective-permute-start.3 = (s32[1]{0:T(128)}, s32[1]{0:T(128)}, u32[]{:S(2)}, u32[]{:S(2)}) collective-permute-start(s32[1]{0:T(128)} %param.10), channel_id=1, source_target_pairs={{0,2},{2,4},{4,6},{6,8},{8,10},{10,12},{12,14},{14,0},{1,3},{3,5},... | collective-permute-start | bytes 20 | tf_op jit(solution)/shard_map/ppermute | solution.py:37
  12.8 1.4 %fusion.86 = (s32[1]{0:T(128)}, s32[1]{0:T(128)}) fusion(s32[9]{0:T(128)} %param.11, s32[]{:T(128)S(6)} %select_n.150, s32[]{:T(128)S(6)} %select_n.151), kind=kLoop, calls=%fused_computation.177 | loop fusion | bytes 24 | tf_op jit(solution)/shard_map/dynamic_slice | solution.py:93
  17.6 1.2 copy.35
  18.8 0.8 dynamic-slice_bitcast_fusion.1
  20.0 0.7 fusion.63
  21.1 1.7 %fusion.80 = (f32[1,128,1536]{1,2,0:T(8,128)}, f32[1,128,1536]{1,2,0:T(8,128)}) fusion(f32[1536]{0:T(1024)S(1)} %get-tuple-element.69, f32[1536]{0:T(1024)S(1)} %get-tuple-element.70, f32[128]{0:T(128)S(1)} %add_rsqrt_fusion.7, f32[128]{0:T(128)S(1)} %broadcast_multiply_fusion.3, bf16[1,128,1536]{1,2,0:T(8,128)(2,1)S(1)} %copy.35), kind=kLoop, calls=%fused_computation.171 | loop fusion | flops 1179648 | bytes 1979392 | tf_op jit(solution)/shard_map/mul | solution.py:48
  22.8 1.8 %reduce_sum.154 = f32[128,12]{0,1:T(8,128)} reduce(f32[128,12,128]{0,2,1:T(8,128)} %bitcast.241, f32[]{:T(128)} %constant.129.clone.1), dimensions={2}, to_apply=%region_2.3 | reduce | flops 195072 | bytes 792580 | tf_op jit(solution)/shard_map/reduce_sum | solution.py:48
  24.6 1.3 %fusion.73 = (f32[128]{0:T(128)}, f32[128]{0:T(128)}) fusion(f32[12,128]{1,0:T(8,128)} %param.14, s32[]{:T(128)S(6)} %select_n.161, s32[]{:T(128)S(6)} %select_n.155), kind=kLoop, calls=%fused_computation.154 | loop fusion | bytes 2056 | tf_op jit(solution)/shard_map/mul | solution.py:49
  25.9 0.7 add_rsqrt_fusion.3
  27.9 1.0 fusion.68
  28.9 0.5 fusion.74
  29.4 0.6 pad_clamp_fusion.1
  30.0 1.5 %fusion.44 = f32[1,3,1536]{2,0,1:T(1,128)} fusion(bf16[3,3,1536]{2,1,0:T(4,128)(2,1)} %copy-done.8, s32[]{:T(128)} %bitcast.41), kind=kOutput, calls=%fused_computation.89 | convolution fusion | flops 27651 | bytes 46084 | tf_op jit(solution)/shard_map/bs,sjd->bjd/dot_general | solution.py:67
  31.5 7.0 %pad_maximum_fusion = bf16[2,2,3,256,1536]{4,3,2,1,0:T(8,128)(2,1)} fusion(bf16[2,2,1,256,1536]{4,3,2,1,0:T(8,128)(2,1)} %collective-permute-done.1, bf16[2,2,1,256,1536]{4,3,2,1,0:T(8,128)(2,1)S(1)} %bitcast.238, bf16[2,2,1,256,1536]{4,3,2,1,0:T(8,128)(2,1)} %collective-permute-done), kind=kLoop, calls=%fused_computation.8 | loop fusion | flops 9437184 | bytes 18874368 | tf_op jit(solution)/shard_map/concatenate | solution.py:31
  38.5 6.5 %slice_bitcast_fusion.2 = (bf16[6,128,1536]{2,1,0:T(8,128)(2,1)S(1)}, bf16[6,128,1536]{2,1,0:T(8,128)(2,1)}, bf16[6,128,1536]{2,1,0:T(8,128)(2,1)}, bf16[6,128,1536]{2,1,0:T(8,128)(2,1)}) fusion(bf16[2,2,6,128,1536]{4,3,2,1,0:T(8,128)(2,1)} %bitcast.235), kind=kLoop, calls=%fused_computation.11 | loop fusion | bytes 18874368 | tf_op jit(solution)/shard_map/squeeze | solution.py:70
  45.0 3.3 %gather_fusion.2 = bf16[2,128,1536]{2,1,0:T(8,128)(2,1)} fusion(bf16[6,128,1536]{2,1,0:T(8,128)(2,1)} %get-tuple-element.47, s32[1024]{0:T(1024)} %pad_clamp_fusion.1), kind=kCustom, calls=%fused_computation.2 | custom fusion | bytes 1572872 | tf_op jit(solution)/shard_map/gather | solution.py:51
  48.2 2.2 %copy.40 = bf16[2,128,1536]{1,0,2:T(2,128)(2,1)S(1)} copy(bf16[2,128,1536]{2,1,0:T(8,128)(2,1)} %gather_fusion.2) | data formatting | bytes 1572864 | tf_op jit(solution)/shard_map/gather | solution.py:51
  50.5 1.4 %reshape.917 = bf16[256,12,128]{0,2,1:T(8,128)(2,1)} reshape(bf16[2,128,1536]{1,0,2:T(2,128)(2,1)S(1)} %copy.40) | data formatting | bytes 1572864 | tf_op jit(solution)/shard_map/reshape.50
  51.9 2.4 %gather_fusion.3 = bf16[2,128,1536]{2,1,0:T(8,128)(2,1)S(1)} fusion(bf16[6,128,1536]{2,1,0:T(8,128)(2,1)} %get-tuple-element.46, s32[1024]{0:T(1024)} %pad_clamp_fusion.1), kind=kCustom, calls=%fused_computation.3 | custom fusion | bytes 1572872 | tf_op jit(solution)/shard_map/gather | solution.py:50
  54.3 1.5 %reshape.1052 = bf16[256,12,128]{2,1,0:T(8,128)(2,1)} reshape(bf16[2,128,1536]{2,1,0:T(8,128)(2,1)S(1)} %gather_fusion.3) | data formatting | bytes 1572864 | tf_op jit(solution)/shard_map/reshape.47
  55.8 3.3 %gather_fusion = bf16[2,128,1536]{2,1,0:T(8,128)(2,1)} fusion(bf16[6,128,1536]{2,1,0:T(8,128)(2,1)} %get-tuple-element.48, s32[1024]{0:T(1024)} %pad_clamp_fusion.1), kind=kCustom, calls=%fused_computation | custom fusion | bytes 1572872 | tf_op jit(solution)/shard_map/gather | solution.py:51
  59.1 2.2 %copy.36 = bf16[2,128,1536]{1,0,2:T(2,128)(2,1)S(1)} copy(bf16[2,128,1536]{2,1,0:T(8,128)(2,1)} %gather_fusion) | data formatting | bytes 1572864 | tf_op jit(solution)/shard_map/gather | solution.py:51
  61.4 1.4 %reshape.913 = bf16[256,12,128]{0,2,1:T(8,128)(2,1)} reshape(bf16[2,128,1536]{1,0,2:T(2,128)(2,1)S(1)} %copy.36) | data formatting | bytes 1572864 | tf_op jit(solution)/shard_map/reshape.15
  62.7 0.7 gather_fusion.1
  63.5 1.6 %reshape.1051 = bf16[256,12,128]{2,1,0:T(8,128)(2,1)} reshape(bf16[2,128,1536]{2,1,0:T(8,128)(2,1)S(1)} %gather_fusion.1) | data formatting | bytes 1572864 | tf_op jit(solution)/shard_map/reshape.12
  65.0 2.0 %fusion.87 = (f32[12,128]{1,0:T(8,128)S(1)}, f32[12,128,256]{2,1,0:T(8,128)S(1)}) fusion(bf16[256,12,128]{2,1,0:T(8,128)(2,1)} %reshape.1051, f32[128,12,128]{0,2,1:T(8,128)} %bitcast.239, f32[128]{0:T(128)} %get-tuple-element.56, f32[128,12]{0,1:T(8,128)S(1)} %add_rsqrt_fusion.3), kind=kOutput, calls=%fused_computation.178 | convolution fusion | flops 102038016 | bytes 3158528 | tf_op jit(solution)/shard_map/bqhd,bkhd->bhqk/dot_general | solution.py:52
  67.1 0.5 fusion
  67.6 0.6 copy-done.5
  69.4 2.0 %fusion.85 = (f32[1,128,1536]{1,2,0:T(8,128)}, f32[1,128,1536]{1,2,0:T(8,128)}) fusion(f32[1536]{0:T(1024)S(1)} %copy-done.11, f32[1536]{0:T(1024)S(1)} %copy-done.10, f32[128]{0:T(128)S(1)} %add_rsqrt_fusion.6, f32[128]{0:T(128)S(1)} %broadcast_multiply_fusion.2, f32[1,128,12,128]{1,3,2,0:T(8,128)S(1)} %fusion.8, f32[1536]{0:T(1024)S(1)} %get-tuple-element.71, ...), kind=kLoop, calls=%fused_computation.176 | loop fusion | flops 1769472 | bytes 2771969 | tf_op jit(solution)/shard_map/mul | solution.py:48
  71.4 1.2 reduce_sum.159
  72.6 2.0 %fusion.88 = (f32[12,128]{1,0:T(8,128)S(1)}, f32[12,128,256]{2,1,0:T(8,128)S(1)}) fusion(bf16[256,12,128]{2,1,0:T(8,128)(2,1)} %reshape.1052, f32[128,12,128]{0,2,1:T(8,128)} %bitcast.244, f32[128]{0:T(128)} %get-tuple-element.55, f32[128,12]{0,1:T(8,128)S(1)} %add_rsqrt_fusion.2), kind=kOutput, calls=%fused_computation.179 | convolution fusion | flops 102038016 | bytes 3158528 | tf_op jit(solution)/shard_map/bqhd,bkhd->bhqk/dot_general | solution.py:52
  74.6 0.5 fusion.2
  75.2 0.6 copy-done.3
  76.5 1.2 %fusion.22 = bf16[1,128,1536]{1,2,0:T(8,128)(2,1)} fusion(f32[1,128,12,128]{1,3,2,0:T(8,128)S(1)} %fusion.9, f32[1536]{0:T(1024)S(1)} %copy-done.9, pred[]{:T(512)} %bitcast, f32[1,128,12,128]{1,3,2,0:T(8,128)S(1)} %fusion.8, f32[1536]{0:T(1024)S(1)} %get-tuple-element.71, bf16[1,128,1536]{1,2,0:T(8,128)(2,1)S(1)} %copy.35, pred[]{:T(512)} %bitcast.1), kind=kLoop, calls=%fused_computation.57 | loop fusion | flops 1572864 | bytes 2371586 | tf_op jit(solution)/shard_map/convert_element_type | solution.py:77
  77.7 1.5 %collective-permute-start.2 = (bf16[1,128,1536]{1,2,0:T(8,128)(2,1)}, bf16[1,128,1536]{1,2,0:T(8,128)(2,1)S(1)}, u32[]{:S(2)}, u32[]{:S(2)}) collective-permute-start(bf16[1,128,1536]{1,2,0:T(8,128)(2,1)} %fusion.22), channel_id=1, source_target_pairs={{0,2},{2,4},{4,6},{6,8},{8,10},{10,12},{12,14},{14,0},{1,3},{3,5},... | collective-permute-start | bytes 1179656 | tf_op jit(solution)/shard_map/ppermute | solution.py:37
  79.4 0.7 fusion.55
  80.1 3.1 %gather_fusion.6 = bf16[2,128,1536]{2,1,0:T(8,128)(2,1)} fusion(bf16[6,128,1536]{2,1,0:T(8,128)(2,1)} %get-tuple-element.47, s32[1024]{0:T(1024)S(1)} %pad_clamp_fusion), kind=kCustom, calls=%fused_computation.6 | custom fusion | bytes 1572872 | tf_op jit(solution)/shard_map/gather | solution.py:51
  83.2 2.4 %gather_fusion.7 = bf16[2,128,1536]{2,1,0:T(8,128)(2,1)S(1)} fusion(bf16[6,128,1536]{2,1,0:T(8,128)(2,1)} %get-tuple-element.46, s32[1024]{0:T(1024)} %copy-done.17), kind=kCustom, calls=%fused_computation.7 | custom fusion | bytes 1572872 | tf_op jit(solution)/shard_map/gather | solution.py:50
  85.6 3.3 %gather_fusion.4 = bf16[2,128,1536]{2,1,0:T(8,128)(2,1)} fusion(bf16[6,128,1536]{2,1,0:T(8,128)(2,1)} %get-tuple-element.48, s32[1024]{0:T(1024)} %copy-done.17), kind=kCustom, calls=%fused_computation.4 | custom fusion | bytes 1572872 | tf_op jit(solution)/shard_map/gather | solution.py:51
  88.9 1.6 %gather_fusion.5 = bf16[2,128,1536]{2,1,0:T(8,128)(2,1)} fusion(bf16[6,128,1536]{2,1,0:T(8,128)(2,1)S(1)} %get-tuple-element.45, s32[1024]{0:T(1024)} %copy-done.17), kind=kCustom, calls=%fused_computation.5 | custom fusion | bytes 1572872 | tf_op jit(solution)/shard_map/gather | solution.py:50
  90.5 2.2 %copy.48 = bf16[2,128,1536]{1,0,2:T(2,128)(2,1)S(1)} copy(bf16[2,128,1536]{2,1,0:T(8,128)(2,1)} %gather_fusion.6) | data formatting | bytes 1572864 | tf_op jit(solution)/shard_map/gather | solution.py:51
  92.7 1.4 %reshape.925 = bf16[256,12,128]{0,2,1:T(8,128)(2,1)} reshape(bf16[2,128,1536]{1,0,2:T(2,128)(2,1)S(1)} %copy.48) | data formatting | bytes 1572864 | tf_op jit(solution)/shard_map/reshape.85
  94.1 0.5 reshape.1054
  94.7 2.3 %copy.44 = bf16[2,128,1536]{1,0,2:T(2,128)(2,1)S(1)} copy(bf16[2,128,1536]{2,1,0:T(8,128)(2,1)} %gather_fusion.4) | data formatting | bytes 1572864 | tf_op jit(solution)/shard_map/gather | solution.py:51
  97.0 1.4 %reshape.921 = bf16[256,12,128]{0,2,1:T(8,128)(2,1)} reshape(bf16[2,128,1536]{1,0,2:T(2,128)(2,1)S(1)} %copy.44) | data formatting | bytes 1572864 | tf_op jit(solution)/shard_map/reshape.68
  98.4 0.5 reshape.1053
  99.4 1.4 %fusion.81 = (f32[1,128,1536]{1,2,0:T(8,128)}, f32[1,128,1536]{1,2,0:T(8,128)S(1)}) fusion(f32[1536]{0:T(1024)S(1)} %copy-done.14, f32[1536]{0:T(1024)S(1)} %copy-done.15, f32[128]{0:T(128)S(1)} %add_rsqrt_fusion.5, f32[128]{0:T(128)S(1)} %broadcast_multiply_fusion.1, bf16[1,128,1536]{1,2,0:T(8,128)(2,1)S(1)} %collective-permute-done.2), kind=kLoop, calls=%fused_computation.172 | loop fusion | flops 1179648 | bytes 1979392 | tf_op jit(solution)/shard_map/mul | solution.py:48
  100.8 1.2 reduce_sum.164
  102.0 0.6 fusion.89
  102.6 0.5 fusion.4
  103.1 0.6 copy-done.4
  103.7 0.5 fusion.10
  104.9 1.8 %fusion.84 = (f32[1,128,1536]{1,2,0:T(8,128)}, f32[1,128,1536]{1,2,0:T(8,128)S(1)}) fusion(f32[1536]{0:T(1024)S(1)} %copy-done.13, f32[1536]{0:T(1024)S(1)} %copy-done.12, f32[128]{0:T(128)S(1)} %add_rsqrt_fusion.4, f32[128]{0:T(128)S(1)} %broadcast_multiply_fusion, f32[1,128,12,128]{1,3,2,0:T(8,128)S(1)} %fusion.10, f32[1536]{0:T(1024)S(1)} %get-tuple-element.74, ...), kind=kLoop, calls=%fused_computation.175 | loop fusion | flops 1769472 | bytes 2771969 | tf_op jit(solution)/shard_map/mul | solution.py:48
  106.7 1.2 reduce_sum.169
  108.0 0.6 fusion.90
  108.5 0.5 fusion.6
  109.1 0.6 copy-done.2
  109.7 0.5 fusion.11
  110.6 1.6 %collective-permute-start.5 = (bf16[1,128,1536]{1,2,0:T(8,128)(2,1)S(1)}, bf16[1,128,1536]{1,2,0:T(8,128)(2,1)S(1)}, u32[]{:S(2)}, u32[]{:S(2)}) collective-permute-start(bf16[1,128,1536]{1,2,0:T(8,128)(2,1)S(1)} %fusion.23), channel_id=1, source_target_pairs={{0,2},{2,4},{4,6},{6,8},{8,10},{10,12},{12,14},{14,0},{1,3},{3,5},... | collective-permute-start | bytes 1179656 | tf_op jit(solution)/shard_map/ppermute | solution.py:37
  112.2 9.1 %collective-permute-done.5 = bf16[1,128,1536]{1,2,0:T(8,128)(2,1)S(1)} collective-permute-done((bf16[1,128,1536]{1,2,0:T(8,128)(2,1)S(1)}, bf16[1,128,1536]{1,2,0:T(8,128)(2,1)S(1)}, u32[]{:S(2)}, u32[]{:S(2)}) %collective-permute-start.5) | collective-permute-done | bytes 393248 | tf_op jit(solution)/shard_map/ppermute | solution.py:37
  121.3 0.9 copy.52
  (69 shorter events, 4.4 us)
Async XLA Ops:
  0.0 31.5 %collective-permute-start.1 = (bf16[2,2,1,256,1536]{4,3,2,1,0:T(8,128)(2,1)}, bf16[2,2,1,256,1536]{4,3,2,1,0:T(8,128)(2,1)}, u32[]{:S(2)}, u32[]{:S(2)}) collective-permute-start(bf16[2,2,1,256,1536]{4,3,2,1,0:T(8,128)(2,1)} %bitcast.236), channel_id=1, source_target_pairs={{1,0},{3,2},{5,4},{7,6},{9,8},{11,10},{13,12},{15,14},{17,16},{19,... | collective-permute-start | bytes 9437192 | tf_op jit(solution)/shard_map/ppermute | solution.py:30
  1.3 30.2 %collective-permute-start = (bf16[2,2,1,256,1536]{4,3,2,1,0:T(8,128)(2,1)}, bf16[2,2,1,256,1536]{4,3,2,1,0:T(8,128)(2,1)}, u32[]{:S(2)}, u32[]{:S(2)}) collective-permute-start(bf16[2,2,1,256,1536]{4,3,2,1,0:T(8,128)(2,1)} %bitcast.237), channel_id=1, source_target_pairs={{0,1},{2,3},{4,5},{6,7},{8,9},{10,11},{12,13},{14,15},{16,17},{18,... | collective-permute-start | bytes 9437192 | tf_op jit(solution)/shard_map/ppermute | solution.py:29
  7.6 18.9 %collective-permute-start.4 = (s32[1]{0:T(128)}, s32[1]{0:T(128)}, u32[]{:S(2)}, u32[]{:S(2)}) collective-permute-start(s32[1]{0:T(128)} %param.9), channel_id=1, source_target_pairs={{0,2},{2,4},{4,6},{6,8},{8,10},{10,12},{12,14},{14,0},{1,3},{3,5},... | collective-permute-start | bytes 20 | tf_op jit(solution)/shard_map/ppermute | solution.py:37
  10.6 16.6 %collective-permute-start.3 = (s32[1]{0:T(128)}, s32[1]{0:T(128)}, u32[]{:S(2)}, u32[]{:S(2)}) collective-permute-start(s32[1]{0:T(128)} %param.10), channel_id=1, source_target_pairs={{0,2},{2,4},{4,6},{6,8},{8,10},{10,12},{12,14},{14,0},{1,3},{3,5},... | collective-permute-start | bytes 20 | tf_op jit(solution)/shard_map/ppermute | solution.py:37
  19.7 1.2 copy-start.6
  19.7 1.2 copy-start.8
  20.9 10.6 %copy-start = (bf16[1,2,2,256,1536]{4,3,2,1,0:T(8,128)(2,1)S(1)}, bf16[1,2,2,256,1536]{4,3,2,1,0:T(8,128)(2,1)}, u32[]{:S(2)}) copy-start(bf16[1,2,2,256,1536]{4,3,2,1,0:T(8,128)(2,1)} %param.15) | copy-start | bytes 9437188
  67.1 1.1 copy-start.5
  68.7 0.7 copy-start.10
  68.7 0.7 copy-start.11
  74.6 1.1 copy-start.3
  75.8 0.7 copy-start.9
  76.3 2.9 %copy-start.20 = (s32[2]{0:T(128)S(1)}, s32[2]{0:T(128)}, u32[]{:S(2)}) copy-start(s32[2]{0:T(128)} %get-tuple-element.68) | copy-start | bytes 28
  76.3 2.9 %copy-start.7 = (bf16[3,3,1536]{2,1,0:T(4,128)(2,1)S(1)}, bf16[3,3,1536]{2,1,0:T(4,128)(2,1)}, u32[]{:S(2)}) copy-start(bf16[3,3,1536]{2,1,0:T(4,128)(2,1)} %copy-done.6) | copy-start | bytes 82948
  76.3 3.1 %copy-start.16 = (f32[1,3,1536]{2,0,1:T(1,128)S(1)}, f32[1,3,1536]{2,0,1:T(1,128)}, u32[]{:S(2)}) copy-start(f32[1,3,1536]{2,0,1:T(1,128)} %fusion.44) | copy-start | bytes 55300
  77.7 21.3 %collective-permute-start.2 = (bf16[1,128,1536]{1,2,0:T(8,128)(2,1)}, bf16[1,128,1536]{1,2,0:T(8,128)(2,1)S(1)}, u32[]{:S(2)}, u32[]{:S(2)}) collective-permute-start(bf16[1,128,1536]{1,2,0:T(8,128)(2,1)} %fusion.22), channel_id=1, source_target_pairs={{0,2},{2,4},{4,6},{6,8},{8,10},{10,12},{12,14},{14,0},{1,3},{3,5},... | collective-permute-start | bytes 1179656 | tf_op jit(solution)/shard_map/ppermute | solution.py:37
  79.2 0.8 copy-start.17
  94.7 3.8 %copy-start.1 = (bf16[2,128,1536]{2,1,0:T(8,128)(2,1)S(1)}, bf16[2,128,1536]{2,1,0:T(8,128)(2,1)}, u32[]{:S(2)}) copy-start(bf16[2,128,1536]{2,1,0:T(8,128)(2,1)} %gather_fusion.5) | copy-start | bytes 2359300
  98.4 1.0 copy-start.14
  98.4 1.0 copy-start.15
  99.2 2.8 %copy-start.19 = (f32[128]{0:T(128)S(1)}, f32[128]{0:T(128)}, u32[]{:S(2)}) copy-start(f32[128]{0:T(128)} %get-tuple-element.56) | copy-start | bytes 1540
  102.6 1.1 copy-start.4
  104.2 0.7 copy-start.12
  104.2 0.7 copy-start.13
  104.9 3.0 %copy-start.18 = (f32[128]{0:T(128)S(1)}, f32[128]{0:T(128)}, u32[]{:S(2)}) copy-start(f32[128]{0:T(128)} %get-tuple-element.55) | copy-start | bytes 1540
  108.5 1.1 copy-start.2
  110.6 10.7 %collective-permute-start.5 = (bf16[1,128,1536]{1,2,0:T(8,128)(2,1)S(1)}, bf16[1,128,1536]{1,2,0:T(8,128)(2,1)S(1)}, u32[]{:S(2)}, u32[]{:S(2)}) collective-permute-start(bf16[1,128,1536]{1,2,0:T(8,128)(2,1)S(1)} %fusion.23), channel_id=1, source_target_pairs={{0,2},{2,4},{4,6},{6,8},{8,10},{10,12},{12,14},{14,0},{1,3},{3,5},... | collective-permute-start | bytes 1179656 | tf_op jit(solution)/shard_map/ppermute | solution.py:37
where the time goes:
time: 124 us; the launch traced here: 122 us
  local copies, waits for them, and re-layouts  54.9 us (44%)
  other arithmetic  28.1 us (23%)
  starting transfers between devices  15.2 us (12%)
  waiting for transfers between devices  9.12 us (7%)
  matrix products  9.11 us (7%)
  between operations  5.86 us (5%)
    gather x8, local copies, waits for them, and re-layouts, attend(): value_tiles[tile_choice].reshape(batch_size, NB * TILE, HEADS, HDIM)  22.1 us
    another operation x8, local copies, waits for them, and re-layouts  9.75 us
    ppermute x4, waiting for transfers between devices, from_behind(): lax.ppermute(x, axis, [(i, (i + by) % devices) for i in range(devices)])  9.11 us
    ppermute x4, starting transfers between devices, from_behind(): lax.ppermute(x, axis, [(i, (i + by) % devices) for i in range(devices)])  7.57 us
    gather x4, local copies, waits for them, and re-layouts, attend(): key_tiles[tile_choice].reshape(batch_size, NB * TILE, HEADS, HDIM)  7.09 us
    concatenate x1, other arithmetic, extended_2(): x = jnp.concatenate([before, x, after], axis=dim)  6.96 us
    mul x4, other arithmetic, attend(): head_rms = jnp.mean(heads_in * heads_in, axis=-1, keepdims=True)  6.79 us
    squeeze x1, local copies, waits for them, and re-layouts, run_slots(): extended[slot_index, 0]  6.49 us
  transfers between devices with their start and end apart: 6, of which 1 were waited for; matrix products, arithmetic and copies ran while one was open for 27% of the time, Pallas kernels for 0%

commit v1 on v0

v1 whole, which is shorter than its diff:
```python
import functools

import jax
import jax.numpy as jnp
from jax import lax
from jax.experimental import pallas as pl
from jax.experimental.pallas import tpu as pltpu
from jax.sharding import PartitionSpec as P

TICKS = 2
CHUNKS = 2
epsilon = 1e-06
MESH = pl.DeviceIdType.MESH


def window_kernel(
    cycle,
    pos_ref,
    step_ref,
    bounds_ref,
    near_ref,
    mod_ref,
    gain_ref,
    patch_ref,
    kv_ref,
    out_ref,
    own,
    staged,
    other,
    hold,
    fin,
    state,
    queries,
    meta_out,
    meta_in,
    meta_smem,
    table,
    own_sem,
    patch_sem,
    meta_send,
    meta_recv,
    meta_local,
    kv_send,
    kv_recv,
    state_send,
    state_recv,
):
    slots, _, slab_tiles, tile, width = kv_ref.shape
    chunks, rows = hold.shape[1], hold.shape[2]
    head_dim = gain_ref.shape[1]
    heads = width // head_dim
    pipe = bounds_ref.shape[0] - 1
    steps, layers = mod_ref.shape[0], mod_ref.shape[1]
    segment = lax.axis_index("segment")
    space = lax.axis_index("space")
    onward = lax.rem(segment + 1, cycle)
    behind = lax.rem(segment + cycle - 1, cycle)
    mate = 1 - space

    def own_copy(slot, part):
        return pltpu.make_async_copy(kv_ref.at[slot, part], own[slot][part], own_sem.at[slot, part])

    def kv_copy(tick, slot, part):
        return pltpu.make_async_remote_copy(
            src_ref=staged.at[tick, slot, part],
            dst_ref=other.at[tick, slot, part],
            send_sem=kv_send.at[tick, slot, part],
            recv_sem=kv_recv.at[tick, slot, part],
            device_id={"space": mate},
            device_id_type=MESH,
        )

    def state_copy(tick, chunk, target):
        return pltpu.make_async_remote_copy(
            src_ref=fin.at[tick, chunk],
            dst_ref=target,
            send_sem=state_send.at[tick, chunk],
            recv_sem=state_recv.at[tick, chunk],
            device_id={"segment": onward},
            device_id_type=MESH,
        )

    patch_copy = pltpu.make_async_copy(patch_ref, hold.at[0], patch_sem)
    meta_copy = pltpu.make_async_remote_copy(
        src_ref=meta_out,
        dst_ref=meta_in,
        send_sem=meta_send,
        recv_sem=meta_recv,
        device_id={"segment": onward},
        device_id_type=MESH,
    )
    order = [(slot, part) for slot in range(slots) for part in range(2)]
    for slot, part in order:
        own_copy(slot, part).start()
    patch_copy.start()

    barrier = pltpu.get_barrier_semaphore()
    pl.semaphore_signal(barrier, inc=1, device_id={"segment": onward}, device_id_type=MESH)
    pl.semaphore_signal(barrier, inc=1, device_id={"segment": behind}, device_id_type=MESH)
    pl.semaphore_signal(barrier, inc=1, device_id={"space": mate}, device_id_type=MESH)

    position = pos_ref[0]
    timestep = step_ref[0]
    table[0, 0] = position
    table[0, 1] = timestep
    lane = lax.broadcasted_iota(jnp.int32, meta_out.shape, 1)
    meta_out[...] = jnp.where(lane == 0, position, timestep)
    pl.semaphore_wait(barrier, 3)
    meta_copy.start()

    def wanted_by_mate(pos):
        return lax.rem(near_ref[mate * slab_tiles + pos, 1], slab_tiles)

    mate_tile = wanted_by_mate(position)
    for slot, part in order:
        own_copy(slot, part).wait()
        staged[0, slot, part] = own[slot][part][mate_tile]
        kv_copy(0, slot, part).start()
    patch_copy.wait()

    section = lax.rem(segment, pipe)
    first_layer = bounds_ref[section]
    layer_count = bounds_ref[section + 1] - first_layer
    to_exp2 = head_dim ** (-0.5) * 1.4426950408889634
    ones = jnp.ones((2 * tile, head_dim), jnp.bfloat16)

    def run(index, carry):
        tick = index // chunks
        chunk = lax.rem(index, chunks)

        @pl.when(index == 1)
        def _():
            meta_copy.wait_recv()
            to_smem = pltpu.make_async_copy(meta_in, meta_smem, meta_local)
            to_smem.start()
            to_smem.wait()
            table[1, 0] = meta_smem[0, 0]
            table[1, 1] = meta_smem[0, 1]
            later_tile = wanted_by_mate(meta_smem[0, 0])
            for slot, part in order:
                staged[1, slot, part] = own[slot][part][later_tile]
                kv_copy(1, slot, part).start()

        @pl.when(tick == 1)
        def _():
            state_copy(0, chunk, hold.at[1, chunk]).wait_recv()

        root = lax.rem(segment - tick + cycle, cycle)
        crossed = jnp.where(lax.rem(root, pipe) + tick >= pipe, 1, 0)
        step_row = jnp.minimum(table[tick, 1] + crossed, steps - 1)
        own_tile = lax.rem(near_ref[space * slab_tiles + table[tick, 0], 0], slab_tiles)
        state[...] = hold[tick, chunk].astype(jnp.float32)

        for slot in range(slots):
            layer = jnp.minimum(first_layer + slot, layers - 1)
            mod = mod_ref[step_row, layer].astype(jnp.float32)
            gain = gain_ref[pl.ds(layer, 1), :]
            active = jnp.where(slot < layer_count, 1.0, 0.0)
            gate = mod[2:3] * active
            spans = [pl.ds(head * head_dim, head_dim) for head in range(heads)]
            total = state[:, spans[0]]
            for span in spans[1:]:
                total = total + state[:, span]
            middle = jnp.sum(total, axis=-1, keepdims=True) * (1.0 / width)
            total = jnp.zeros((rows, head_dim), jnp.float32)
            for span in spans:
                centred = state[:, span] - middle
                total = total + centred * centred
            spread = jnp.sum(total, axis=-1, keepdims=True) * (1.0 / width)
            scale = lax.rsqrt(spread + epsilon)
            for head, span in enumerate(spans):
                cols = slice(head * head_dim, (head + 1) * head_dim)
                normed = (state[:, span] - middle) * scale
                shifted = normed * (1.0 + mod[1:2, cols]) + mod[0:1, cols]
                rms = jnp.sum(shifted * shifted, axis=-1, keepdims=True) * (1.0 / head_dim)
                queries[:, span] = (shifted * lax.rsqrt(rms + epsilon) * gain).astype(jnp.bfloat16)

            @pl.when(chunk == 0)
            def _():
                for part in range(2):
                    kv_copy(tick, slot, part).wait_recv()

            for head, span in enumerate(spans):
                cols = slice(head * head_dim, (head + 1) * head_dim)
                keys = jnp.concatenate(
                    [own[slot][0][own_tile, :, span], other[tick, slot, 0, :, span]], axis=0
                )
                values = jnp.concatenate(
                    [own[slot][1][own_tile, :, span], other[tick, slot, 1, :, span]], axis=0
                )
                scores = lax.dot_general(
                    queries[:, span], keys, (((1,), (1,)), ((), ())), preferred_element_type=jnp.float32
                )
                top = jnp.max(scores, axis=-1, keepdims=True)
                weights = jnp.exp2((scores - top) * to_exp2).astype(jnp.bfloat16)
                blended = lax.dot_general(
                    weights,
                    jnp.concatenate([values, ones], axis=1),
                    (((1,), (0,)), ((), ())),
                    preferred_element_type=jnp.float32,
                )
                state[:, span] += gate[:, cols] * (blended[:, :head_dim] / blended[:, head_dim:])

        fin[tick, chunk] = state[...].astype(jnp.bfloat16)

        @pl.when(tick == 0)
        def _():
            state_copy(0, chunk, hold.at[1, chunk]).start()

        @pl.when(tick == 1)
        def _():
            state_copy(1, chunk, out_ref.at[chunk]).start()

        return carry

    lax.fori_loop(0, TICKS * chunks, run, 0)

    meta_copy.wait_send()
    for tick in range(TICKS):
        for slot, part in order:
            kv_copy(tick, slot, part).wait_send()
    for chunk in range(chunks):
        state_copy(0, chunk, hold.at[1, chunk]).wait_send()
        state_copy(1, chunk, out_ref.at[chunk]).wait()


def per_device(
    patches, positions, timesteps, section_bounds, tile_neighbours, modulation, query_gain, stale_kv
):
    _, tile, width = patches.shape
    _, slots, _, slab_rows, _ = stale_kv.shape
    slab_tiles = slab_rows // tile
    rows = tile // CHUNKS
    cycle = lax.axis_size("segment")
    kv = stale_kv.reshape(slots, 2, slab_tiles, tile, width)
    smem = pl.BlockSpec(memory_space=pltpu.SMEM)
    vmem = pl.BlockSpec(memory_space=pltpu.VMEM)
    anywhere = pl.BlockSpec(memory_space=pl.ANY)
    dma = pltpu.SemaphoreType.DMA
    flops = TICKS * slots * 4 * tile * 2 * tile * width
    advanced = pl.pallas_call(
        functools.partial(window_kernel, cycle),
        out_shape=jax.ShapeDtypeStruct((CHUNKS, rows, width), patches.dtype),
        in_specs=[smem, smem, smem, smem, vmem, vmem, anywhere, anywhere],
        out_specs=anywhere,
        scratch_shapes=[
            [[pltpu.VMEM(kv.shape[2:], kv.dtype) for _ in range(2)] for _ in range(slots)],
            pltpu.VMEM((TICKS, slots, 2, tile, width), kv.dtype),
            pltpu.VMEM((TICKS, slots, 2, tile, width), kv.dtype),
            pltpu.VMEM((TICKS, CHUNKS, rows, width), jnp.bfloat16),
            pltpu.VMEM((TICKS, CHUNKS, rows, width), jnp.bfloat16),
            pltpu.VMEM((rows, width), jnp.float32),
            pltpu.VMEM((rows, width), jnp.bfloat16),
            pltpu.VMEM((8, 128), jnp.int32),
            pltpu.VMEM((8, 128), jnp.int32),
            pltpu.SMEM((8, 128), jnp.int32),
            pltpu.SMEM((TICKS, 2), jnp.int32),
            dma((slots, 2)),
            dma,
            dma,
            dma,
            dma,
            dma((TICKS, slots, 2)),
            dma((TICKS, slots, 2)),
            dma((TICKS, CHUNKS)),
            dma((TICKS, CHUNKS)),
        ],
        compiler_params=pltpu.CompilerParams(
            collective_id=0, has_side_effects=True, vmem_limit_bytes=58 * 2**20
        ),
        cost_estimate=pl.CostEstimate(
            flops=flops, bytes_accessed=kv.size * 2 + patches.size * 4, transcendentals=0
        ),
    )(
        positions,
        timesteps,
        section_bounds,
        tile_neighbours,
        modulation,
        query_gain,
        patches.reshape(CHUNKS, rows, width),
        kv,
    )
    return advanced.reshape(patches.shape)


def solution(mesh):
    placed = (
        P(("groups", "segment"), "space", None),
        P(("groups", "segment")),
        P(("groups", "segment")),
        P(),
        P(),
        P("groups", None, None, None),
        P(),
        P(("groups", "segment"), None, None, "space", None),
    )
    return jax.shard_map(
        per_device,
        mesh=mesh,
        in_specs=placed,
        out_specs=P(("groups", "segment"), "space", None),
        check_vma=False,
    )
```

time: 124 us -> 35.3 us (0.28); the launches traced: 122 us -> 35.1 us
  local copies, waits for them, and re-layouts: 54.9 us -> 3.1 us
  Pallas kernels: 0 us -> 30.7 us
  other arithmetic: 28.1 us -> 0 us
  starting transfers between devices: 15.2 us -> 0 us
  waiting for transfers between devices: 9.12 us -> 0 us
  matrix products: 9.11 us -> 0 us
  between operations: 5.86 us -> 1.31 us
    pallas_call x0 -> x1, Pallas kernels: none -> 30.7 us  [per_device(): pl.pallas_call(functools.partial(window_kernel, cycle), out_shape=jax.Sha...]
    gather x13 -> x0, local copies, waits for them, and re-layouts: 30.1 us -> none  [the longest x8 22.1 us: attend(): value_tiles[tile_choice].reshape(batch_size, NB * TILE, HEADS, HDIM)]
    ppermute x6 -> x0, starting transfers between devices: 15.2 us -> none  [the longest x4 7.57 us: from_behind(): lax.ppermute(x, axis, [(i, (i + by) % devices) for i in range(devices)])]
    another operation x8 -> x0, local copies, waits for them, and re-layouts: 9.75 us -> none
    reduce_sum x16 -> x0, other arithmetic: 9.41 us -> none  [the longest x4 5.33 us: attend(): head_rms = jnp.mean(heads_in * heads_in, axis=-1, keepdims=True)]
    ppermute x6 -> x0, waiting for transfers between devices: 9.12 us -> none  [the longest x4 9.11 us: from_behind(): lax.ppermute(x, axis, [(i, (i + by) % devices) for i in range(devices)])]
    dot_general x12 -> x0, matrix products: 9.11 us -> none  [the longest x4 5.23 us: attend(): jnp.einsum('bqhd,bkhd->bhqk', queries, key_rows, preferred_element_type=j...]
    squeeze x2 -> x0, local copies, waits for them, and re-layouts: 7.31 us -> none  [the longest x1 6.49 us: run_slots(): extended[slot_index, 0]]
  transfers between devices with their start and end apart: 6 -> 0, of which waited for: 1 -> 0; matrix products, arithmetic and copies ran while one was open for 27% -> 0% of each run, Pallas kernels for 0% -> 0%
where the time goes in v1:
time: 35.3 us; the launch traced here: 35.1 us
  Pallas kernels  30.7 us (87%)
  local copies, waits for them, and re-layouts  3.1 us (9%)
  between operations  1.31 us (4%)
    pallas_call x1, Pallas kernels, per_device(): pl.pallas_call(functools.partial(window_kernel, cycle), out_shape=jax.Sha...  30.7 us
    unnamed x2, local copies, waits for them, and re-layouts  3.1 us

profile of v1, /device:TPU:0, one launch (start us, length us, event | category | flops | bytes accessed | tf_op | source)
XLA Modules:
  0.0 35.1 jit_solution(4717461256290818956)
XLA Ops:
  1.3 1.3 %copy.9.near_ref = s32[4,2]{1,0:T(4,128)} copy(s32[4,2]{0,1:T(2,128)} %param.12) | data formatting | bytes 64 | tf_op args[4]
  2.6 30.7 %shard_map.82 = bf16[2,64,1536]{2,1,0:T(8,128)(2,1)} custom-call(s32[1]{0:T(128)S(6)} %copy.11.pos_ref, s32[1]{0:T(128)S(6)} %copy.12.step_ref, s32[9]{0:T(128)} %bounds_ref.1, s32[4,2]{1,0:T(4,128)} %copy.9.near_ref, bf16[3,12,3,1536]{3,2,1,0:T(4,128)(2,1)} %mod_ref.1, f32[12,128]{1,0:T(8,128)} %gain_ref.1, bf16[2,64,1536]{2,1,0:T(8,128)(2,1)} %bitcast.5, ...), custom_call_target="tpu_custom_call" | custom-call | flops 805306368 | bytes 3932160 | tf_op jit(solution)/shard_map/pallas_call | solution.py:241
  33.4 1.8 %copy.13 = bf16[1,128,1536]{2,1,0:T(8,128)(2,1)} copy(bf16[1,128,1536]{2,1,0:T(8,128)(2,1)} %bitcast.4) | data formatting | bytes 786432

commit v2 on v1

--- a/solution.py
+++ b/solution.py
@@ -95,7 +95,6 @@
     patch_copy.start()
 
     barrier = pltpu.get_barrier_semaphore()
-    pl.semaphore_signal(barrier, inc=1, device_id={"segment": onward}, device_id_type=MESH)
     pl.semaphore_signal(barrier, inc=1, device_id={"segment": behind}, device_id_type=MESH)
     pl.semaphore_signal(barrier, inc=1, device_id={"space": mate}, device_id_type=MESH)
 
@@ -105,11 +104,11 @@
     table[0, 1] = timestep
     lane = lax.broadcasted_iota(jnp.int32, meta_out.shape, 1)
     meta_out[...] = jnp.where(lane == 0, position, timestep)
-    pl.semaphore_wait(barrier, 3)
+    pl.semaphore_wait(barrier, 2)
     meta_copy.start()
 
     def wanted_by_mate(pos):
-        return lax.rem(near_ref[mate * slab_tiles + pos, 1], slab_tiles)
+        return lax.rem(near_ref[1, mate * slab_tiles + pos], slab_tiles)
 
     mate_tile = wanted_by_mate(position)
     for slot, part in order:
@@ -148,7 +147,7 @@
         root = lax.rem(segment - tick + cycle, cycle)
         crossed = jnp.where(lax.rem(root, pipe) + tick >= pipe, 1, 0)
         step_row = jnp.minimum(table[tick, 1] + crossed, steps - 1)
-        own_tile = lax.rem(near_ref[space * slab_tiles + table[tick, 0], 0], slab_tiles)
+        own_tile = lax.rem(near_ref[0, space * slab_tiles + table[tick, 0]], slab_tiles)
         state[...] = hold[tick, chunk].astype(jnp.float32)
 
         for slot in range(slots):
@@ -266,7 +265,7 @@
             dma((TICKS, CHUNKS)),
         ],
         compiler_params=pltpu.CompilerParams(
-            collective_id=0, has_side_effects=True, vmem_limit_bytes=58 * 2**20
+            collective_id=0, has_side_effects=True, vmem_limit_bytes=52 * 2**20
         ),
         cost_estimate=pl.CostEstimate(
             flops=flops, bytes_accessed=kv.size * 2 + patches.size * 4, transcendentals=0
@@ -275,7 +274,7 @@
         positions,
         timesteps,
         section_bounds,
-        tile_neighbours,
+        tile_neighbours.T,
         modulation,
         query_gain,
         patches.reshape(CHUNKS, rows, width),

time: 35.3 us -> 36.7 us (1.040)
  local copies, waits for them, and re-layouts: 3.1 us -> 4.78 us
  Pallas kernels: 30.7 us -> 30.3 us
    unnamed x2 -> x11, local copies, waits for them, and re-layouts: 3.1 us -> 4.78 us
    pallas_call x1, Pallas kernels: 30.7 us -> 30.3 us  [per_device(): pl.pallas_call(functools.partial(window_kernel, cycle), out_shape=jax.Sha...]
where the time goes in v2:
time: 36.7 us; the launch traced here: 36.4 us
  Pallas kernels  30.3 us (83%)
  local copies, waits for them, and re-layouts  4.78 us (13%)
  between operations  1.32 us (4%)
    pallas_call x1, Pallas kernels, per_device(): pl.pallas_call(functools.partial(window_kernel, cycle), out_shape=jax.Sha...  30.3 us
    unnamed x11, local copies, waits for them, and re-layouts  4.78 us

profile of v2, /device:TPU:0, one launch (start us, length us, event | category | flops | bytes accessed | tf_op | source)
XLA Modules:
  0.0 36.4 jit_solution(445215559839452185)
XLA Ops:
  1.3 0.0 copy-start
  1.3 1.0 %copy-done = bf16[3,12,3,1536]{3,2,1,0:T(4,128)(2,1)S(1)} copy-done((bf16[3,12,3,1536]{3,2,1,0:T(4,128)(2,1)S(1)}, bf16[3,12,3,1536]{3,2,1,0:T(4,128)(2,1)}, u32[]{:S(2)}) %copy-start) | copy-done | bytes 331800
  2.3 0.0 copy-start.1
  2.3 1.0 %copy-done.1 = bf16[1,128,1536]{2,1,0:T(8,128)(2,1)S(1)} copy-done((bf16[1,128,1536]{2,1,0:T(8,128)(2,1)S(1)}, bf16[1,128,1536]{2,1,0:T(8,128)(2,1)}, u32[]{:S(2)}) %copy-start.1) | copy-done | bytes 393240
  3.3 0.0 copy-start.2
  3.3 0.7 %copy-done.2 = f32[12,128]{1,0:T(8,128)S(1)} copy-done((f32[12,128]{1,0:T(8,128)S(1)}, f32[12,128]{1,0:T(8,128)}, u32[]{:S(2)}) %copy-start.2) | copy-done | bytes 6168
  4.0 0.0 copy-start.3
  4.0 0.7 %copy-done.3 = s32[4,2]{0,1:T(2,128)S(1)} copy-done((s32[4,2]{0,1:T(2,128)S(1)}, s32[4,2]{0,1:T(2,128)}, u32[]{:S(2)}) %copy-start.3) | copy-done | bytes 56
  4.7 0.0 copy-start.4
  4.7 0.7 %copy-done.4 = s32[9]{0:T(128)S(1)} copy-done((s32[9]{0:T(128)S(1)}, s32[9]{0:T(128)}, u32[]{:S(2)}) %copy-start.4) | copy-done | bytes 60
  5.3 30.3 %shard_map.82 = bf16[2,64,1536]{2,1,0:T(8,128)(2,1)S(1)} custom-call(s32[1]{0:T(128)S(6)} %copy.10.pos_ref, s32[1]{0:T(128)S(6)} %copy.11.step_ref, s32[9]{0:T(128)S(1)} %copy-done.4, s32[2,4]{1,0:T(2,128)S(1)} %bitcast.6, bf16[3,12,3,1536]{3,2,1,0:T(4,128)(2,1)S(1)} %copy-done, f32[12,128]{1,0:T(8,128)S(1)} %copy-done.2, bf16[2,64,1536]{2,1,0:T(8,128)(2,1)S(1)} %bitcast.5, ...), custom_call_target="tpu_custom_call" | custom-call | flops 805306368 | bytes 3932160 | tf_op jit(solution)/shard_map/pallas_call | solution.py:240
  35.7 0.7 %copy.12 = bf16[1,128,1536]{2,1,0:T(8,128)(2,1)} copy(bf16[1,128,1536]{2,1,0:T(8,128)(2,1)S(1)} %bitcast.4) | data formatting | bytes 786432
Async XLA Ops:
  1.3 1.0 %copy-start = (bf16[3,12,3,1536]{3,2,1,0:T(4,128)(2,1)S(1)}, bf16[3,12,3,1536]{3,2,1,0:T(4,128)(2,1)}, u32[]{:S(2)}) copy-start(bf16[3,12,3,1536]{3,2,1,0:T(4,128)(2,1)} %mod_ref.1) | copy-start | bytes 995332
  2.3 1.0 %copy-start.1 = (bf16[1,128,1536]{2,1,0:T(8,128)(2,1)S(1)}, bf16[1,128,1536]{2,1,0:T(8,128)(2,1)}, u32[]{:S(2)}) copy-start(bf16[1,128,1536]{2,1,0:T(8,128)(2,1)} %param.8) | copy-start | bytes 1179652
  3.3 0.7 %copy-start.2 = (f32[12,128]{1,0:T(8,128)S(1)}, f32[12,128]{1,0:T(8,128)}, u32[]{:S(2)}) copy-start(f32[12,128]{1,0:T(8,128)} %gain_ref.1) | copy-start | bytes 18436
  4.0 0.7 %copy-start.3 = (s32[4,2]{0,1:T(2,128)S(1)}, s32[4,2]{0,1:T(2,128)}, u32[]{:S(2)}) copy-start(s32[4,2]{0,1:T(2,128)} %param.12) | copy-start | bytes 100
  4.7 0.7 %copy-start.4 = (s32[9]{0:T(128)S(1)}, s32[9]{0:T(128)}, u32[]{:S(2)}) copy-start(s32[9]{0:T(128)} %bounds_ref.1) | copy-start | bytes 112

commit v3 on v2

--- a/solution.py
+++ b/solution.py
@@ -8,7 +8,7 @@
 from jax.sharding import PartitionSpec as P
 
 TICKS = 2
-CHUNKS = 2
+CHUNKS = 4
 epsilon = 1e-06
 MESH = pl.DeviceIdType.MESH
 
@@ -19,11 +19,13 @@
     step_ref,
     bounds_ref,
     near_ref,
-    mod_ref,
-    gain_ref,
+    mod_hbm,
+    gain_hbm,
     patch_ref,
     kv_ref,
     out_ref,
+    mod_ref,
+    gain_ref,
     own,
     staged,
     other,
@@ -36,6 +38,8 @@
     meta_smem,
     table,
     own_sem,
+    mod_sem,
+    gain_sem,
     patch_sem,
     meta_send,
     meta_recv,
@@ -81,6 +85,8 @@
         )
 
     patch_copy = pltpu.make_async_copy(patch_ref, hold.at[0], patch_sem)
+    mod_copy = pltpu.make_async_copy(mod_hbm, mod_ref, mod_sem)
+    gain_copy = pltpu.make_async_copy(gain_hbm, gain_ref, gain_sem)
     meta_copy = pltpu.make_async_remote_copy(
         src_ref=meta_out,
         dst_ref=meta_in,
@@ -93,6 +99,8 @@
     for slot, part in order:
         own_copy(slot, part).start()
     patch_copy.start()
+    mod_copy.start()
+    gain_copy.start()
 
     barrier = pltpu.get_barrier_semaphore()
     pl.semaphore_signal(barrier, inc=1, device_id={"segment": behind}, device_id_type=MESH)
@@ -116,6 +124,8 @@
         staged[0, slot, part] = own[slot][part][mate_tile]
         kv_copy(0, slot, part).start()
     patch_copy.wait()
+    mod_copy.wait()
+    gain_copy.wait()
 
     section = lax.rem(segment, pipe)
     first_layer = bounds_ref[section]
@@ -233,16 +243,18 @@
     cycle = lax.axis_size("segment")
     kv = stale_kv.reshape(slots, 2, slab_tiles, tile, width)
     smem = pl.BlockSpec(memory_space=pltpu.SMEM)
-    vmem = pl.BlockSpec(memory_space=pltpu.VMEM)
+    hbm = pl.BlockSpec(memory_space=pltpu.HBM)
     anywhere = pl.BlockSpec(memory_space=pl.ANY)
     dma = pltpu.SemaphoreType.DMA
     flops = TICKS * slots * 4 * tile * 2 * tile * width
     advanced = pl.pallas_call(
         functools.partial(window_kernel, cycle),
-        out_shape=jax.ShapeDtypeStruct((CHUNKS, rows, width), patches.dtype),
-        in_specs=[smem, smem, smem, smem, vmem, vmem, anywhere, anywhere],
+        out_shape=pltpu.VMEM((CHUNKS, rows, width), patches.dtype),
+        in_specs=[smem, smem, smem, smem, hbm, hbm, hbm, hbm],
         out_specs=anywhere,
         scratch_shapes=[
+            pltpu.VMEM(modulation.shape, modulation.dtype),
+            pltpu.VMEM(query_gain.shape, query_gain.dtype),
             [[pltpu.VMEM(kv.shape[2:], kv.dtype) for _ in range(2)] for _ in range(slots)],
             pltpu.VMEM((TICKS, slots, 2, tile, width), kv.dtype),
             pltpu.VMEM((TICKS, slots, 2, tile, width), kv.dtype),
@@ -259,13 +271,15 @@
             dma,
             dma,
             dma,
+            dma,
+            dma,
             dma((TICKS, slots, 2)),
             dma((TICKS, slots, 2)),
             dma((TICKS, CHUNKS)),
             dma((TICKS, CHUNKS)),
         ],
         compiler_params=pltpu.CompilerParams(
-            collective_id=0, has_side_effects=True, vmem_limit_bytes=52 * 2**20
+            collective_id=0, has_side_effects=True, vmem_limit_bytes=58 * 2**20
         ),
         cost_estimate=pl.CostEstimate(
             flops=flops, bytes_accessed=kv.size * 2 + patches.size * 4, transcendentals=0

time: 36.7 us -> 34 us (0.926)
  local copies, waits for them, and re-layouts: 4.78 us -> 0.75 us
  Pallas kernels: 30.3 us -> 31.8 us
    unnamed x11 -> x1, local copies, waits for them, and re-layouts: 4.78 us -> 0.75 us
    pallas_call x1, Pallas kernels: 30.3 us -> 31.8 us  [per_device(): pl.pallas_call(functools.partial(window_kernel, cycle), out_shape=pltpu.V...]
where the time goes in v3:
time: 34 us; the launch traced here: 33.8 us
  Pallas kernels  31.8 us (94%)
  between operations  1.3 us (4%)
  local copies, waits for them, and re-layouts  0.75 us (2%)
    pallas_call x1, Pallas kernels, per_device(): pl.pallas_call(functools.partial(window_kernel, cycle), out_shape=pltpu.V...  31.8 us
    unnamed x1, local copies, waits for them, and re-layouts  0.75 us

profile of v3, /device:TPU:0, one launch (start us, length us, event | category | flops | bytes accessed | tf_op | source)
XLA Modules:
  0.0 33.8 jit_solution(4181618319256085246)
XLA Ops:
  1.3 31.8 %shard_map.82 = bf16[4,32,1536]{2,1,0:T(8,128)(2,1)S(1)} custom-call(s32[1]{0:T(128)S(6)} %copy.11.pos_ref, s32[1]{0:T(128)S(6)} %copy.12.step_ref, s32[9]{0:T(128)} %bounds_ref.1, s32[2,4]{1,0:T(2,128)} %bitcast.7, bf16[3,12,3,1536]{3,2,1,0:T(4,128)(2,1)} %mod_hbm.1, f32[12,128]{1,0:T(8,128)} %gain_hbm.1, bf16[4,32,1536]{2,1,0:T(8,128)(2,1)} %bitcast.6, ...), custom_call_target="tpu_custom_call" | custom-call | flops 805306368 | bytes 3932160 | tf_op jit(solution)/shard_map/pallas_call | solution.py:250
  33.1 0.7 %copy.10 = bf16[1,128,1536]{2,1,0:T(8,128)(2,1)} copy(bf16[1,128,1536]{2,1,0:T(8,128)(2,1)S(1)} %bitcast.4) | data formatting | bytes 786432

commit v4 on v3

--- a/solution.py
+++ b/solution.py
@@ -8,7 +8,8 @@
 from jax.sharding import PartitionSpec as P
 
 TICKS = 2
-CHUNKS = 4
+CHUNKS = 2
+AHEAD = 3
 epsilon = 1e-06
 MESH = pl.DeviceIdType.MESH
 
@@ -131,7 +132,6 @@
     first_layer = bounds_ref[section]
     layer_count = bounds_ref[section + 1] - first_layer
     to_exp2 = head_dim ** (-0.5) * 1.4426950408889634
-    ones = jnp.ones((2 * tile, head_dim), jnp.bfloat16)
 
     def run(index, carry):
         tick = index // chunks
@@ -189,26 +189,43 @@
                 for part in range(2):
                     kv_copy(tick, slot, part).wait_recv()
 
-            for head, span in enumerate(spans):
+            def score(head):
+                keys = jnp.concatenate(
+                    [own[slot][0][own_tile, :, spans[head]], other[tick, slot, 0, :, spans[head]]], axis=0
+                )
+                return lax.dot_general(
+                    queries[:, spans[head]], keys, (((1,), (1,)), ((), ())), preferred_element_type=jnp.float32
+                )
+
+            def weigh(scores):
+                top = jnp.max(scores, axis=-1, keepdims=True)
+                powers = jnp.exp2((scores - top) * to_exp2)
+                total = jnp.sum(powers, axis=-1, keepdims=True)
+                guess = pl.reciprocal(total, approx=True)
+                return powers.astype(jnp.bfloat16), guess * (2.0 - total * guess)
+
+            def blend(head, weights):
+                values = jnp.concatenate(
+                    [own[slot][1][own_tile, :, spans[head]], other[tick, slot, 1, :, spans[head]]], axis=0
+                )
+                return lax.dot_general(
+                    weights, values, (((1,), (0,)), ((), ())), preferred_element_type=jnp.float32
+                )
+
+            def settle(head, blended, inverse):
                 cols = slice(head * head_dim, (head + 1) * head_dim)
-                keys = jnp.concatenate(
-                    [own[slot][0][own_tile, :, span], other[tick, slot, 0, :, span]], axis=0
-                )
-                values = jnp.concatenate(
-                    [own[slot][1][own_tile, :, span], other[tick, slot, 1, :, span]], axis=0
-                )
-                scores = lax.dot_general(
-                    queries[:, span], keys, (((1,), (1,)), ((), ())), preferred_element_type=jnp.float32
-                )
-                top = jnp.max(scores, axis=-1, keepdims=True)
-                weights = jnp.exp2((scores - top) * to_exp2).astype(jnp.bfloat16)
-                blended = lax.dot_general(
-                    weights,
-                    jnp.concatenate([values, ones], axis=1),
-                    (((1,), (0,)), ((), ())),
-                    preferred_element_type=jnp.float32,
-                )
-                state[:, span] += gate[:, cols] * (blended[:, :head_dim] / blended[:, head_dim:])
+                state[:, spans[head]] += gate[:, cols] * (blended * inverse)
+
+            ahead = [score(head) for head in range(min(AHEAD, heads))]
+            mixing = []
+            for head in range(heads):
+                if head + AHEAD < heads:
+                    ahead.append(score(head + AHEAD))
+                weights, inverse = weigh(ahead[head])
+                mixing.append((blend(head, weights), inverse))
+                if head >= 1:
+                    settle(head - 1, *mixing[head - 1])
+            settle(heads - 1, *mixing[heads - 1])
 
         fin[tick, chunk] = state[...].astype(jnp.bfloat16)
 

time: 34 us -> 33 us (0.971)
  Pallas kernels: 31.8 us -> 30.8 us
    pallas_call x1, Pallas kernels: 31.8 us -> 30.8 us  [per_device(): pl.pallas_call(functools.partial(window_kernel, cycle), out_shape=pltpu.V...]
where the time goes in v4:
time: 33 us; the launch traced here: 32.8 us
  Pallas kernels  30.8 us (93%)
  between operations  1.3 us (4%)
  local copies, waits for them, and re-layouts  0.75 us (2%)
    pallas_call x1, Pallas kernels, per_device(): pl.pallas_call(functools.partial(window_kernel, cycle), out_shape=pltpu.V...  30.8 us
    unnamed x1, local copies, waits for them, and re-layouts  0.75 us

profile of v4, /device:TPU:0, one launch (start us, length us, event | category | flops | bytes accessed | tf_op | source)
XLA Modules:
  0.0 32.8 jit_solution(1297296452289597408)
XLA Ops:
  1.3 30.8 %shard_map.82 = bf16[2,64,1536]{2,1,0:T(8,128)(2,1)S(1)} custom-call(s32[1]{0:T(128)S(6)} %copy.11.pos_ref, s32[1]{0:T(128)S(6)} %copy.12.step_ref, s32[9]{0:T(128)} %bounds_ref.1, s32[2,4]{1,0:T(2,128)} %bitcast.7, bf16[3,12,3,1536]{3,2,1,0:T(4,128)(2,1)} %mod_hbm.1, f32[12,128]{1,0:T(8,128)} %gain_hbm.1, bf16[2,64,1536]{2,1,0:T(8,128)(2,1)} %bitcast.6, ...), custom_call_target="tpu_custom_call" | custom-call | flops 805306368 | bytes 3932160 | tf_op jit(solution)/shard_map/pallas_call | solution.py:267
  32.1 0.7 %copy.10 = bf16[1,128,1536]{2,1,0:T(8,128)(2,1)} copy(bf16[1,128,1536]{2,1,0:T(8,128)(2,1)S(1)} %bitcast.4) | data formatting | bytes 786432

commit v5 on v4

--- a/solution.py
+++ b/solution.py
@@ -33,6 +33,8 @@
     hold,
     fin,
     state,
+    bent,
+    squares,
     queries,
     meta_out,
     meta_in,
@@ -133,6 +135,8 @@
     layer_count = bounds_ref[section + 1] - first_layer
     to_exp2 = head_dim ** (-0.5) * 1.4426950408889634
 
+    ones = jnp.ones((2 * tile, head_dim), jnp.bfloat16)
+
     def run(index, carry):
         tick = index // chunks
         chunk = lax.rem(index, chunks)
@@ -181,8 +185,12 @@
                 cols = slice(head * head_dim, (head + 1) * head_dim)
                 normed = (state[:, span] - middle) * scale
                 shifted = normed * (1.0 + mod[1:2, cols]) + mod[0:1, cols]
-                rms = jnp.sum(shifted * shifted, axis=-1, keepdims=True) * (1.0 / head_dim)
-                queries[:, span] = (shifted * lax.rsqrt(rms + epsilon) * gain).astype(jnp.bfloat16)
+                bent[:, span] = shifted
+                squares[pl.ds(head * rows, rows), :] = (shifted * shifted).astype(jnp.bfloat16)
+            square_sums = jnp.dot(squares[...], ones[:head_dim], preferred_element_type=jnp.float32)
+            for head, span in enumerate(spans):
+                rms = square_sums[head * rows : (head + 1) * rows] * (1.0 / head_dim)
+                queries[:, span] = (bent[:, span] * lax.rsqrt(rms + epsilon) * gain).astype(jnp.bfloat16)
 
             @pl.when(chunk == 0)
             def _():
@@ -199,33 +207,35 @@
 
             def weigh(scores):
                 top = jnp.max(scores, axis=-1, keepdims=True)
-                powers = jnp.exp2((scores - top) * to_exp2)
-                total = jnp.sum(powers, axis=-1, keepdims=True)
-                guess = pl.reciprocal(total, approx=True)
-                return powers.astype(jnp.bfloat16), guess * (2.0 - total * guess)
+                return jnp.exp2((scores - top) * to_exp2).astype(jnp.bfloat16)
 
             def blend(head, weights):
                 values = jnp.concatenate(
                     [own[slot][1][own_tile, :, spans[head]], other[tick, slot, 1, :, spans[head]]], axis=0
                 )
                 return lax.dot_general(
-                    weights, values, (((1,), (0,)), ((), ())), preferred_element_type=jnp.float32
+                    weights,
+                    jnp.concatenate([values, ones], axis=1),
+                    (((1,), (0,)), ((), ())),
+                    preferred_element_type=jnp.float32,
                 )
 
-            def settle(head, blended, inverse):
+            def settle(head, mixed):
                 cols = slice(head * head_dim, (head + 1) * head_dim)
-                state[:, spans[head]] += gate[:, cols] * (blended * inverse)
+                total = mixed[:, head_dim:]
+                guess = pl.reciprocal(total, approx=True)
+                inverse = guess * (2.0 - total * guess)
+                state[:, spans[head]] += gate[:, cols] * (mixed[:, :head_dim] * inverse)
 
             ahead = [score(head) for head in range(min(AHEAD, heads))]
             mixing = []
             for head in range(heads):
                 if head + AHEAD < heads:
                     ahead.append(score(head + AHEAD))
-                weights, inverse = weigh(ahead[head])
-                mixing.append((blend(head, weights), inverse))
+                mixing.append(blend(head, weigh(ahead[head])))
                 if head >= 1:
-                    settle(head - 1, *mixing[head - 1])
-            settle(heads - 1, *mixing[heads - 1])
+                    settle(head - 1, mixing[head - 1])
+            settle(heads - 1, mixing[heads - 1])
 
         fin[tick, chunk] = state[...].astype(jnp.bfloat16)
 
@@ -278,6 +288,8 @@
             pltpu.VMEM((TICKS, CHUNKS, rows, width), jnp.bfloat16),
             pltpu.VMEM((TICKS, CHUNKS, rows, width), jnp.bfloat16),
             pltpu.VMEM((rows, width), jnp.float32),
+            pltpu.VMEM((rows, width), jnp.float32),
+            pltpu.VMEM((width // query_gain.shape[1] * rows, query_gain.shape[1]), jnp.bfloat16),
             pltpu.VMEM((rows, width), jnp.bfloat16),
             pltpu.VMEM((8, 128), jnp.int32),
             pltpu.VMEM((8, 128), jnp.int32),

time: 33 us -> 32.6 us (0.988)
  Pallas kernels: 30.8 us -> 30.3 us
    pallas_call x1, Pallas kernels: 30.8 us -> 30.3 us  [per_device(): pl.pallas_call(functools.partial(window_kernel, cycle), out_shape=pltpu.V...]
where the time goes in v5:
time: 32.6 us; the launch traced here: 32.4 us
  Pallas kernels  30.3 us (93%)
  between operations  1.3 us (4%)
  local copies, waits for them, and re-layouts  0.75 us (2%)
    pallas_call x1, Pallas kernels, per_device(): pl.pallas_call(functools.partial(window_kernel, cycle), out_shape=pltpu.V...  30.3 us
    unnamed x1, local copies, waits for them, and re-layouts  0.75 us

profile of v5, /device:TPU:0, one launch (start us, length us, event | category | flops | bytes accessed | tf_op | source)
XLA Modules:
  0.0 32.4 jit_solution(6973104041282906739)
XLA Ops:
  1.3 30.3 %shard_map.82 = bf16[2,64,1536]{2,1,0:T(8,128)(2,1)S(1)} custom-call(s32[1]{0:T(128)S(6)} %copy.11.pos_ref, s32[1]{0:T(128)S(6)} %copy.12.step_ref, s32[9]{0:T(128)} %bounds_ref.1, s32[2,4]{1,0:T(2,128)} %bitcast.7, bf16[3,12,3,1536]{3,2,1,0:T(4,128)(2,1)} %mod_hbm.1, f32[12,128]{1,0:T(8,128)} %gain_hbm.1, bf16[2,64,1536]{2,1,0:T(8,128)(2,1)} %bitcast.6, ...), custom_call_target="tpu_custom_call" | custom-call | flops 805306368 | bytes 3932160 | tf_op jit(solution)/shard_map/pallas_call | solution.py:277
  31.6 0.7 %copy.10 = bf16[1,128,1536]{2,1,0:T(8,128)(2,1)} copy(bf16[1,128,1536]{2,1,0:T(8,128)(2,1)S(1)} %bitcast.4) | data formatting | bytes 786432

commit v6 on v5

--- a/solution.py
+++ b/solution.py
@@ -141,19 +141,6 @@
         tick = index // chunks
         chunk = lax.rem(index, chunks)
 
-        @pl.when(index == 1)
-        def _():
-            meta_copy.wait_recv()
-            to_smem = pltpu.make_async_copy(meta_in, meta_smem, meta_local)
-            to_smem.start()
-            to_smem.wait()
-            table[1, 0] = meta_smem[0, 0]
-            table[1, 1] = meta_smem[0, 1]
-            later_tile = wanted_by_mate(meta_smem[0, 0])
-            for slot, part in order:
-                staged[1, slot, part] = own[slot][part][later_tile]
-                kv_copy(1, slot, part).start()
-
         @pl.when(tick == 1)
         def _():
             state_copy(0, chunk, hold.at[1, chunk]).wait_recv()
@@ -196,6 +183,20 @@
             def _():
                 for part in range(2):
                     kv_copy(tick, slot, part).wait_recv()
+
+            @pl.when(index == 0)
+            def _():
+                if slot == 0:
+                    meta_copy.wait_recv()
+                    to_smem = pltpu.make_async_copy(meta_in, meta_smem, meta_local)
+                    to_smem.start()
+                    to_smem.wait()
+                    table[1, 0] = meta_smem[0, 0]
+                    table[1, 1] = meta_smem[0, 1]
+                later_tile = wanted_by_mate(meta_smem[0, 0])
+                for part in range(2):
+                    staged[1, slot, part] = own[slot][part][later_tile]
+                    kv_copy(1, slot, part).start()
 
             def score(head):
                 keys = jnp.concatenate(

time: 32.6 us -> 33.2 us (1.018)
  Pallas kernels: 30.3 us -> 31 us
    pallas_call x1, Pallas kernels: 30.3 us -> 31 us  [per_device(): pl.pallas_call(functools.partial(window_kernel, cycle), out_shape=pltpu.V...]
where the time goes in v6:
time: 33.2 us; the launch traced here: 33 us
  Pallas kernels  31 us (93%)
  between operations  1.3 us (4%)
  local copies, waits for them, and re-layouts  0.75 us (2%)
    pallas_call x1, Pallas kernels, per_device(): pl.pallas_call(functools.partial(window_kernel, cycle), out_shape=pltpu.V...  31 us
    unnamed x1, local copies, waits for them, and re-layouts  0.75 us

profile of v6, /device:TPU:0, one launch (start us, length us, event | category | flops | bytes accessed | tf_op | source)
XLA Modules:
  0.0 33.0 jit_solution(18103005158625468350)
XLA Ops:
  1.3 31.0 %shard_map.82 = bf16[2,64,1536]{2,1,0:T(8,128)(2,1)S(1)} custom-call(s32[1]{0:T(128)S(6)} %copy.11.pos_ref, s32[1]{0:T(128)S(6)} %copy.12.step_ref, s32[9]{0:T(128)} %bounds_ref.1, s32[2,4]{1,0:T(2,128)} %bitcast.7, bf16[3,12,3,1536]{3,2,1,0:T(4,128)(2,1)} %mod_hbm.1, f32[12,128]{1,0:T(8,128)} %gain_hbm.1, bf16[2,64,1536]{2,1,0:T(8,128)(2,1)} %bitcast.6, ...), custom_call_target="tpu_custom_call" | custom-call | flops 805306368 | bytes 3932160 | tf_op jit(solution)/shard_map/pallas_call | solution.py:278
  32.3 0.7 %copy.10 = bf16[1,128,1536]{2,1,0:T(8,128)(2,1)} copy(bf16[1,128,1536]{2,1,0:T(8,128)(2,1)S(1)} %bitcast.4) | data formatting | bytes 786432

commit v7 on v5

--- a/solution.py
+++ b/solution.py
@@ -122,10 +122,14 @@
         return lax.rem(near_ref[1, mate * slab_tiles + pos], slab_tiles)
 
     mate_tile = wanted_by_mate(position)
-    for slot, part in order:
-        own_copy(slot, part).wait()
-        staged[0, slot, part] = own[slot][part][mate_tile]
-        kv_copy(0, slot, part).start()
+
+    def send_first(slot):
+        for part in range(2):
+            own_copy(slot, part).wait()
+            staged[0, slot, part] = own[slot][part][mate_tile]
+            kv_copy(0, slot, part).start()
+
+    send_first(0)
     patch_copy.wait()
     mod_copy.wait()
     gain_copy.wait()
@@ -191,6 +195,9 @@
             for head, span in enumerate(spans):
                 rms = square_sums[head * rows : (head + 1) * rows] * (1.0 / head_dim)
                 queries[:, span] = (bent[:, span] * lax.rsqrt(rms + epsilon) * gain).astype(jnp.bfloat16)
+
+            if slot + 1 < slots:
+                pl.when(index == 0)(functools.partial(send_first, slot + 1))
 
             @pl.when(chunk == 0)
             def _():

time: 32.6 us -> 32.6 us (level)
  no operation moved by 1% of the time
where the time goes in v7:
time: 32.6 us; the launch traced here: 32.4 us
  Pallas kernels  30.4 us (93%)
  between operations  1.3 us (4%)
  local copies, waits for them, and re-layouts  0.75 us (2%)
    pallas_call x1, Pallas kernels, per_device(): pl.pallas_call(functools.partial(window_kernel, cycle), out_shape=pltpu.V...  30.4 us
    unnamed x1, local copies, waits for them, and re-layouts  0.75 us

profile of v7, /device:TPU:0, one launch (start us, length us, event | category | flops | bytes accessed | tf_op | source)
XLA Modules:
  0.0 32.4 jit_solution(4054060224091104675)
XLA Ops:
  1.3 30.4 %shard_map.82 = bf16[2,64,1536]{2,1,0:T(8,128)(2,1)S(1)} custom-call(s32[1]{0:T(128)S(6)} %copy.11.pos_ref, s32[1]{0:T(128)S(6)} %copy.12.step_ref, s32[9]{0:T(128)} %bounds_ref.1, s32[2,4]{1,0:T(2,128)} %bitcast.7, bf16[3,12,3,1536]{3,2,1,0:T(4,128)(2,1)} %mod_hbm.1, f32[12,128]{1,0:T(8,128)} %gain_hbm.1, bf16[2,64,1536]{2,1,0:T(8,128)(2,1)} %bitcast.6, ...), custom_call_target="tpu_custom_call" | custom-call | flops 805306368 | bytes 3932160 | tf_op jit(solution)/shard_map/pallas_call | solution.py:284
  31.7 0.7 %copy.10 = bf16[1,128,1536]{2,1,0:T(8,128)(2,1)} copy(bf16[1,128,1536]{2,1,0:T(8,128)(2,1)S(1)} %bitcast.4) | data formatting | bytes 786432
